TPU v7x, 256 devices: a whole 4x4x8 slice. The times are simulated.
256 devices in a mesh: island: 16 (over x, z_lo), expert: 4 (over y), fsdp: 4 (over z_hi, core).
Axes of the slice: x: 4, y: 4, z: 8 (z_hi: 2, z_lo: 4; z = z_hi * 4 + z_lo), core: 2. Of those that a mesh axis runs over, the one named last changes fastest.
Arguments:
- deltas: bfloat16 [16, 4, 4096, 1536], P('island', 'expert', 'fsdp'), may hold values from -6 to 6
- order: int32 [4], replicated, may hold values from 0 to 15
- staleness: int32 [16], replicated, may hold values from 0 to 15
- period: int32 [1], replicated, may hold values from 2 to 4
- counter: int32 [1], replicated, may hold values from 0 to 11
- theta: float32 [4, 4096, 1536], P('expert', ('fsdp', 'island')), may hold values from -6 to 6
- momentum: float32 [4, 4096, 1536], P('expert', ('fsdp', 'island')), may hold values from -4 to 4
- accum: float32 [4, 4096, 1536], P('expert', ('fsdp', 'island')), may hold values from -4 to 4
Outputs:
- fresh: bfloat16 [16, 4, 4096, 1536], P('island', 'expert', 'fsdp')
- theta_out: float32 [4, 4096, 1536], P('expert', ('fsdp', 'island'))
- momentum_out: float32 [4, 4096, 1536], P('expert', ('fsdp', 'island'))
- accum_out: float32 [4, 4096, 1536], P('expert', ('fsdp', 'island'))
All inputs are finite; a program needn't handle non-finite values.
Results may differ from a plain program's by a relative error of at most 0.001.
Values may be sent and summed in bfloat16 or wider, within the bound.
A program may use at most 128 MiB of HBM per device.

v0:
```python
import jax
import jax.numpy as jnp
from jax import lax
from jax.sharding import PartitionSpec as P


def spread(shard, axis, root):
    mine = lax.axis_index(axis) == root
    return lax.psum(jnp.where(mine, shard, jnp.zeros_like(shard)), axis)


def local(deltas, order, staleness, period, counter, theta, momentum, accum):
    rate = 0.7
    beta = 0.9
    islands = lax.axis_size("island")
    myself = lax.axis_index("island")
    mine = deltas[0]
    exp_loc, rows_all, width = mine.shape
    rows = rows_all // islands
    period_f = period[0].astype(jnp.float32)
    fresh = jnp.zeros(mine.shape, jnp.bfloat16)
    for k in range(order.shape[0]):
        source = order[k]
        whole = spread(mine, "island", source)
        piece = lax.dynamic_slice_in_dim(whole, myself * rows, rows, 1)
        weight = lax.rsqrt(1.0 + staleness[source].astype(jnp.float32) + k)
        grad = weight * piece.astype(jnp.float32)
        boundary = (counter[0] + k + 1) % period[0] == 0
        correction = 1.0 - jnp.power(jnp.float32(beta), (counter[0] + k + 1).astype(jnp.float32))
        momentum = jnp.where(boundary, beta * momentum + accum / period_f, momentum)
        accum = jnp.where(boundary, grad, accum + grad)
        theta = theta - rate * (
            grad + jnp.where(boundary, beta * momentum / correction, jnp.float32(0.0))
        )
        rounded = theta.astype(jnp.bfloat16)
        gathered = lax.all_gather(rounded, "island", axis=1, tiled=True)
        fresh = jnp.where(myself == source, gathered, fresh)
    return (fresh[None], theta, momentum, accum)


def solution(mesh):
    placed = (
        P("island", "expert", "fsdp", None),
        P(),
        P(),
        P(),
        P(),
        P("expert", ("fsdp", "island"), None),
        P("expert", ("fsdp", "island"), None),
        P("expert", ("fsdp", "island"), None),
    )
    return jax.shard_map(
        local,
        mesh=mesh,
        in_specs=placed,
        out_specs=(
            P("island", "expert", "fsdp", None),
            P("expert", ("fsdp", "island"), None),
            P("expert", ("fsdp", "island"), None),
            P("expert", ("fsdp", "island"), None),
        ),
        check_vma=False,
    )
```

profile of v0, /device:TPU:24, one launch (start us, length us, event | category | flops | bytes accessed | tf_op | source)
XLA Modules:
  0.0 954.0 jit_solution(10924398924033915100)
XLA Ops:
  7.2 0.0 all-reduce.3.cloned.1.call-start
  7.2 1.5 fusion.5
  11.3 6.2 select_bitcast_fusion.1
  17.4 0.0 copy-start.2
  17.4 0.0 all-reduce.3.cloned.1.call-update
  17.5 0.0 all-gather.5.cloned.1.call-start
  26.7 0.7 fusion.4
  30.4 537.1 %all-reduce.3.cloned.1.call-done = (bf16[1,1024,1536]{2,1,0:T(8,128)(2,1)}, bf16[1,1024,1536]{2,1,0:T(8,128)(2,1)}, bf16[1,1024,1536]{2,1,0:T(8,128)(2,1)}, bf16[1,1024,1536]{2,1,0:T(8,128)(2,1)}) async-done(((bf16[1,1024,1536]{2,1,0:T(8,128)(2,1)}, bf16[1,1024,1536]{2,1,0:T(8,128)(2,1)}, bf16[1,1024,1536]{2,1,0:T(8,128)(2,1)}, bf16[1,1024,1536]{2,1,0:T(8,128)(2,1)}), (bf16[1,1024,1536]{2,1,0:T(8,128)(2,1)}, ...) | async-done | bytes 12582928 | tf_op jit(solution)/shard_map/psum | solution.py:9
  567.5 1.8 fusion.1
  569.3 2.4 add_select_fusion
  571.7 2.0 fusion.2
  573.7 2.2 fusion.3
  575.9 0.0 all-gather.5.cloned.1.call-update
  575.9 0.0 all-gather.7.cloned.1.call-start
  576.0 0.7 all-gather.7.cloned.1.call-update
  576.6 0.0 all-gather.9.cloned.1.call-start
  576.7 0.5 all-gather.9.cloned.1.call-update
  577.2 0.0 all-gather.11.cloned.1.call-start
  577.3 0.5 all-gather.11.cloned.1.call-update
  577.8 90.3 %all-gather.5.cloned.1.call-done = bf16[1,1024,1536]{2,1,0:T(8,128)(2,1)} async-done(((bf16[1,64,1536]{2,1,0:T(8,128)(2,1)}), bf16[1,1024,1536]{2,1,0:T(8,128)(2,1)}) %all-gather.5.cloned.1.call-update) | async-done | bytes 3145744 | tf_op jit(solution)/shard_map/all_gather | solution.py:36
  668.1 91.7 %all-gather.7.cloned.1.call-done = bf16[1,1024,1536]{2,1,0:T(8,128)(2,1)} async-done(((bf16[1,64,1536]{2,1,0:T(8,128)(2,1)}), bf16[1,1024,1536]{2,1,0:T(8,128)(2,1)}) %all-gather.7.cloned.1.call-update) | async-done | bytes 3145744 | tf_op jit(solution)/shard_map/all_gather | solution.py:36
  759.8 91.5 %all-gather.9.cloned.1.call-done = bf16[1,1024,1536]{2,1,0:T(8,128)(2,1)} async-done(((bf16[1,64,1536]{2,1,0:T(8,128)(2,1)}), bf16[1,1024,1536]{2,1,0:T(8,128)(2,1)}) %all-gather.9.cloned.1.call-update) | async-done | bytes 3145744 | tf_op jit(solution)/shard_map/all_gather | solution.py:36
  851.3 92.1 %all-gather.11.cloned.1.call-done = bf16[1,1024,1536]{2,1,0:T(8,128)(2,1)} async-done(((bf16[1,64,1536]{2,1,0:T(8,128)(2,1)}), bf16[1,1024,1536]{2,1,0:T(8,128)(2,1)}) %all-gather.11.cloned.1.call-update) | async-done | bytes 3145744 | tf_op jit(solution)/shard_map/all_gather | solution.py:36
  943.4 4.1 select_bitcast_fusion
  (7 shorter events, 0.0 us)
Async XLA Ops:
  7.2 560.3 %all-reduce.3.cloned.1.call-start = ((), (), s32[]{:S(2)}) async-start(), calls=%async_computation.4 | async-start | bytes 25165824 | tf_op jit(solution)/shard_map/psum | solution.py:9
  17.4 9.2 copy-start.3
  17.4 550.1 %copy-start = (f32[1,64,1536]{2,1,0:T(8,128)S(1)}, f32[1,64,1536]{2,1,0:T(8,128)}, u32[]{:S(2)}) copy-start(f32[1,64,1536]{2,1,0:T(8,128)} %param.15) | copy-start | bytes 1179652
  17.4 550.1 %copy-start.1 = (f32[1,64,1536]{2,1,0:T(8,128)S(1)}, f32[1,64,1536]{2,1,0:T(8,128)}, u32[]{:S(2)}) copy-start(f32[1,64,1536]{2,1,0:T(8,128)} %param.14) | copy-start | bytes 1179652
  17.4 550.1 %copy-start.2 = (f32[1,64,1536]{2,1,0:T(8,128)S(1)}, f32[1,64,1536]{2,1,0:T(8,128)}, u32[]{:S(2)}) copy-start(f32[1,64,1536]{2,1,0:T(8,128)} %param.13) | copy-start | bytes 1179652
  17.5 650.6 %all-gather.5.cloned.1.call-start = ((), (), s32[]{:S(2)}) async-start(), calls=%async_computation | async-start | bytes 3342336 | tf_op jit(solution)/shard_map/all_gather | solution.py:36
  575.9 183.9 %all-gather.7.cloned.1.call-start = ((), (), s32[]{:S(2)}) async-start(), calls=%async_computation.1 | async-start | bytes 3342336 | tf_op jit(solution)/shard_map/all_gather | solution.py:36
  576.6 274.6 %all-gather.9.cloned.1.call-start = ((), (), s32[]{:S(2)}) async-start(), calls=%async_computation.2 | async-start | bytes 3342336 | tf_op jit(solution)/shard_map/all_gather | solution.py:36
  577.2 366.2 %all-gather.11.cloned.1.call-start = ((), (), s32[]{:S(2)}) async-start(), calls=%async_computation.3 | async-start | bytes 3342336 | tf_op jit(solution)/shard_map/all_gather | solution.py:36
Sparse Core Ops, SparseCore 0:
  17.6 549.8 all-reduce.2
  576.0 92.0 all-gather.4
  669.9 89.8 all-gather.6
  761.4 89.8 all-gather.8
  853.5 89.8 all-gather.10
where the time goes:
time: 954 us
  waiting for transfers between devices  904 us (95%)
  between operations  28.5 us (3%)
  other arithmetic  18.7 us (2%)
    psum x1, waiting for transfers between devices, spread(): return lax.psum(jnp.where(mine, shard, jnp.zeros_like(shard)), axis)  537 us
    all_gather x4, waiting for transfers between devices, local(): gathered = lax.all_gather(rounded, 'island', axis=1, tiled=True)  366 us
  transfers between devices with their start and end apart: 5, of which 5 were waited for; matrix products, arithmetic and copies ran while one was open for 0% of the time, Pallas kernels for 0%

commit v1 on v0

--- a/solution.py
+++ b/solution.py
@@ -33,7 +33,9 @@
             grad + jnp.where(boundary, beta * momentum / correction, jnp.float32(0.0))
         )
         rounded = theta.astype(jnp.bfloat16)
-        gathered = lax.all_gather(rounded, "island", axis=1, tiled=True)
+        gathered = jnp.concatenate(
+            lax.all_to_all(jnp.stack([rounded] * lax.axis_size("island")), "island", 0, 0), axis=1
+        )
         fresh = jnp.where(myself == source, gathered, fresh)
     return (fresh[None], theta, momentum, accum)
 

time: 954 us -> 888 us (0.931)
  waiting for transfers between devices: 904 us -> 537 us
  blocking collectives: 0 us -> 303 us
    all_gather x4 -> x0, waiting for transfers between devices: 366 us -> none  [local(): gathered = lax.all_gather(rounded, 'island', axis=1, tiled=True)]
    all_to_all x0 -> x4, blocking collectives: none -> 303 us  [local(): lax.all_to_all(jnp.stack([rounded] * lax.axis_size('island')), 'island',...]
  transfers between devices with their start and end apart: 5 -> 1, of which waited for: 5 -> 1; matrix products, arithmetic and copies ran while one was open for 0% -> 0% of each run, Pallas kernels for 0% -> 0%
where the time goes in v1:
time: 888 us
  waiting for transfers between devices  537 us (60%)
  blocking collectives  303 us (34%)
  between operations  28.7 us (3%)
  other arithmetic  15.3 us (2%)
    psum x1, waiting for transfers between devices, spread(): return lax.psum(jnp.where(mine, shard, jnp.zeros_like(shard)), axis)  537 us
    all_to_all x4, blocking collectives, local(): lax.all_to_all(jnp.stack([rounded] * lax.axis_size('island')), 'island',...  303 us
  transfers between devices with their start and end apart: 1, of which 1 were waited for; matrix products, arithmetic and copies ran while one was open for 0% of the time, Pallas kernels for 0%

profile of v1, /device:TPU:24, one launch (start us, length us, event | category | flops | bytes accessed | tf_op | source)
XLA Modules:
  0.0 887.6 jit_solution(2729028770447125908)
XLA Ops:
  7.2 0.0 all-reduce.3.cloned.1.call-start
  7.2 1.5 fusion.1
  11.2 6.1 select_bitcast_fusion
  17.4 0.0 copy-start.2
  17.4 0.0 all-reduce.3.cloned.1.call-update
  26.5 0.0 copy-done.3
  26.5 0.7 fusion
  30.2 537.2 %all-reduce.3.cloned.1.call-done = (bf16[1,1024,1536]{2,1,0:T(8,128)(2,1)}, bf16[1,1024,1536]{2,1,0:T(8,128)(2,1)}, bf16[1,1024,1536]{2,1,0:T(8,128)(2,1)}, bf16[1,1024,1536]{2,1,0:T(8,128)(2,1)}) async-done(((bf16[1,1024,1536]{2,1,0:T(8,128)(2,1)}, bf16[1,1024,1536]{2,1,0:T(8,128)(2,1)}, bf16[1,1024,1536]{2,1,0:T(8,128)(2,1)}, bf16[1,1024,1536]{2,1,0:T(8,128)(2,1)}), (bf16[1,1024,1536]{2,1,0:T(8,128)(2,1)}, ...) | async-done | bytes 12582928 | tf_op jit(solution)/shard_map/psum | solution.py:9
  567.4 0.0 copy-done
  567.4 0.0 copy-done.1
  567.4 0.0 copy-done.2
  567.4 1.1 convert_bitcast_fusion
  568.5 2.4 add_select_fusion
  570.9 1.3 convert_bitcast_fusion.2
  572.2 2.2 convert_bitcast_fusion.3
  574.4 0.3 stack.8
  574.7 77.1 %all_to_all.20 = bf16[16,1,64,1536]{3,2,1,0:T(8,128)(2,1)S(1)} all-to-all(bf16[16,1,64,1536]{3,2,1,0:T(8,128)(2,1)S(1)} %stack.8), channel_id=1, replica_groups=mesh['island'=16,'expert'=4,'fsdp'=4] {'island'}, dimensions={0} | all-to-all | bytes 6291456 | tf_op jit(solution)/shard_map/all_to_all | solution.py:37
  651.8 0.3 stack.9
  652.1 75.5 %all_to_all.21 = bf16[16,1,64,1536]{3,2,1,0:T(8,128)(2,1)S(1)} all-to-all(bf16[16,1,64,1536]{3,2,1,0:T(8,128)(2,1)S(1)} %stack.9), channel_id=1, replica_groups=mesh['island'=16,'expert'=4,'fsdp'=4] {'island'}, dimensions={0} | all-to-all | bytes 6291456 | tf_op jit(solution)/shard_map/all_to_all | solution.py:37
  727.6 0.3 stack.10
  727.9 75.2 %all_to_all.22 = bf16[16,1,64,1536]{3,2,1,0:T(8,128)(2,1)S(1)} all-to-all(bf16[16,1,64,1536]{3,2,1,0:T(8,128)(2,1)S(1)} %stack.10), channel_id=1, replica_groups=mesh['island'=16,'expert'=4,'fsdp'=4] {'island'}, dimensions={0} | all-to-all | bytes 6291456 | tf_op jit(solution)/shard_map/all_to_all | solution.py:37
  803.1 0.3 stack.11
  803.4 75.1 %all_to_all.23 = bf16[16,1,64,1536]{3,2,1,0:T(8,128)(2,1)S(1)} all-to-all(bf16[16,1,64,1536]{3,2,1,0:T(8,128)(2,1)S(1)} %stack.11), channel_id=1, replica_groups=mesh['island'=16,'expert'=4,'fsdp'=4] {'island'}, dimensions={0} | all-to-all | bytes 6291456 | tf_op jit(solution)/shard_map/all_to_all | solution.py:37
  878.5 2.2 select_select_fusion
  (3 shorter events, 0.0 us)
Async XLA Ops:
  7.2 560.2 %all-reduce.3.cloned.1.call-start = ((), (), s32[]{:S(2)}) async-start(), calls=%async_computation.4 | async-start | bytes 25165824 | tf_op jit(solution)/shard_map/psum | solution.py:9
  17.4 9.2 %copy-start.3 = (s32[16]{0:T(128)S(1)}, s32[16]{0:T(128)}, u32[]{:S(2)}) copy-start(s32[16]{0:T(128)} %param.10) | copy-start | bytes 196
  17.4 550.1 %copy-start = (f32[1,64,1536]{2,1,0:T(8,128)S(1)}, f32[1,64,1536]{2,1,0:T(8,128)}, u32[]{:S(2)}) copy-start(f32[1,64,1536]{2,1,0:T(8,128)} %param.15) | copy-start | bytes 1179652
  17.4 550.1 %copy-start.1 = (f32[1,64,1536]{2,1,0:T(8,128)S(1)}, f32[1,64,1536]{2,1,0:T(8,128)}, u32[]{:S(2)}) copy-start(f32[1,64,1536]{2,1,0:T(8,128)} %param.14) | copy-start | bytes 1179652
  17.4 550.1 %copy-start.2 = (f32[1,64,1536]{2,1,0:T(8,128)S(1)}, f32[1,64,1536]{2,1,0:T(8,128)}, u32[]{:S(2)}) copy-start(f32[1,64,1536]{2,1,0:T(8,128)} %param.13) | copy-start | bytes 1179652
Sparse Core Ops, SparseCore 0:
  17.5 549.8 all-reduce.2
